TPU v7x, 32 devices: a whole 2x2x4 slice. The times are simulated.
32 devices in a mesh: energy: 8 (over z, x), atom: 4 (over y, core).
Axes of the slice: x: 2, y: 2, z: 4, core: 2. Of those that a mesh axis runs over, the one named last changes fastest.
Arguments:
- green_blocks: float32 [32, 32, 34, 288], P('energy', 'atom'), may hold values from -6 to 6
- coupling: float32 [32, 12, 12], P('atom'), may hold values from -1.75 to 1.75
- neighbours: int32 [32, 34], P('atom'), may hold values from 0 to 31
- freq_offset: int32 [64], replicated, may hold values from 1 to 2, as said below
- emit_weight: float32 [64], replicated, may hold values from 0.02 to 0.2
- absorb_weight: float32 [64], replicated, may hold values from 0.02 to 0.2
Outputs:
- sigma: float32 [32, 32, 34, 288], P('energy', 'atom')
Inputs may be any that keep to these rules, and one draw needn't show every extreme that they name: `freq_offset`: every offset is 1 or more and at least one offset equals 2.
All inputs are finite; a program needn't handle non-finite values.
Results may differ from a plain program's by a relative error of at most 0.00007.
Values sent between devices are 32-bit elements; how exact they have to be, the bound alone decides.
A program may use at most 128 MiB of HBM per device.

v0:
```python
import functools

import jax
import jax.numpy as jnp
from jax import lax
from jax.experimental import pallas as pl
from jax.experimental.pallas import tpu as pltpu
from jax.sharding import PartitionSpec as P

OFF = 2
LANES = 128
MESH = pl.DeviceIdType.MESH


def kernel(
    energy_count,
    atom_count,
    x_ref,
    coup_ref,
    nbr_ref,
    freq_ref,
    emit_ref,
    absorb_ref,
    out_ref,
    gbuf,
    obuf,
    call,
    right_coef,
    left_coef,
    xt,
    mid,
    ot,
    local_sem,
    out_sem,
    halo_send,
    halo_recv,
    coup_send,
    coup_recv,
):
    rows, nbrs, atoms, width = x_ref.shape
    orb = coup_ref.shape[0]
    cells = orb * orb
    per_tile = LANES // atoms
    tiles = -(-nbrs // per_tile)
    spans = [(t * per_tile, min(per_tile, nbrs - t * per_tile)) for t in range(tiles)]
    order = sorted(range(tiles), key=lambda t: (spans[t][1], t))
    all_atoms = atoms * atom_count

    me_e = lax.axis_index("energy")
    me_a = lax.axis_index("atom")
    has_left = me_e > 0
    has_right = me_e < energy_count - 1

    barrier = pltpu.get_barrier_semaphore()

    def greet(e, a):
        pl.semaphore_signal(barrier, inc=1, device_id=(e, a), device_id_type=MESH)

    @pl.when(has_left)
    def _():
        greet(me_e - 1, me_a)

    @pl.when(has_right)
    def _():
        greet(me_e + 1, me_a)

    partners = [lax.rem(me_a + k, atom_count) for k in range(1, atom_count)]
    for partner in partners:
        greet(me_e, partner)
    inner = jnp.logical_and(has_left, has_right)

    @pl.when(inner)
    def _():
        pl.semaphore_wait(barrier, atom_count + 1)

    @pl.when(jnp.logical_not(inner))
    def _():
        pl.semaphore_wait(barrier, atom_count)

    def halo(t, to_right):
        start, count = spans[t]
        src_row, dst_row, side = (rows - OFF, 0, 0) if to_right else (0, rows + OFF, 1)
        return pltpu.make_async_remote_copy(
            src_ref=x_ref.at[pl.ds(src_row, OFF), pl.ds(start, count)],
            dst_ref=gbuf.at[pl.ds(dst_row, OFF), pl.ds(start, count)],
            send_sem=halo_send.at[side, t],
            recv_sem=halo_recv.at[side, t],
            device_id=(me_e + 1 if to_right else me_e - 1, me_a),
            device_id_type=MESH,
        )

    coup_copies = []
    for k, partner in enumerate(partners):
        copy = pltpu.make_async_remote_copy(
            src_ref=coup_ref,
            dst_ref=call.at[:, pl.ds(pl.multiple_of(me_a * atoms, atoms), atoms)],
            send_sem=coup_send.at[k],
            recv_sem=coup_recv.at[k],
            device_id=(me_e, partner),
            device_id_type=MESH,
        )
        copy.start()
        coup_copies.append(copy)

    for t in order:

        @pl.when(has_right)
        def _():
            halo(t, True).start()

        @pl.when(has_left)
        def _():
            halo(t, False).start()

    local = pltpu.make_async_copy(x_ref, gbuf.at[pl.ds(OFF, rows), pl.ds(0, nbrs)], local_sem)
    local.start()

    call[:, pl.ds(pl.multiple_of(me_a * atoms, atoms), atoms), :] = coup_ref[...]

    @pl.when(jnp.logical_not(has_left))
    def _():
        gbuf[0:OFF] = jnp.zeros((OFF,) + gbuf.shape[1:], jnp.float32)

    @pl.when(jnp.logical_not(has_right))
    def _():
        gbuf[rows + OFF : rows + 2 * OFF] = jnp.zeros((OFF,) + gbuf.shape[1:], jnp.float32)

    freq = freq_ref[...]

    def weight(ref, step):
        return jnp.sum(jnp.where(freq == step, ref[...], 0.0), axis=1, keepdims=True)

    weights = [
        (0, weight(emit_ref, 2)),
        (1, weight(emit_ref, 1)),
        (3, weight(absorb_ref, 1)),
        (4, weight(absorb_ref, 2)),
    ]

    lanes = tiles * LANES
    slot = lax.broadcasted_iota(jnp.int32, (nbrs, lanes), 0)
    pair = lax.broadcasted_iota(jnp.int32, (nbrs, lanes), 1)
    spread = jnp.where(pair // atoms == slot, 1.0, 0.0).astype(jnp.float32)
    listed = jnp.dot(
        nbr_ref[...].astype(jnp.float32), spread, preferred_element_type=jnp.float32, precision=lax.Precision.HIGHEST
    )
    atom_row = lax.broadcasted_iota(jnp.int32, (atoms, lanes), 0)
    atom_pair = lax.broadcasted_iota(jnp.int32, (atoms, lanes), 1)
    own = jnp.where(atom_pair % atoms == atom_row, 1.0, 0.0).astype(jnp.float32)
    index = jnp.sum(listed * own, axis=0, keepdims=True)
    ids = lax.broadcasted_iota(jnp.int32, (all_atoms, lanes), 0).astype(jnp.float32)
    chosen = jnp.where(ids == index, 1.0, 0.0).astype(jnp.float32)

    def expand(source, select, target):
        def one(a, carry):
            table = lax.dot_general(
                source[a],
                select,
                (((0,), (0,)), ((), ())),
                preferred_element_type=jnp.float32,
                precision=lax.Precision.HIGHEST,
            )
            for t in range(tiles):
                for d in range(orb):
                    row = table[d : d + 1, t * LANES : (t + 1) * LANES]
                    target[t, a * orb + d] = jnp.broadcast_to(row, (8, LANES))
            return carry

        lax.fori_loop(0, orb, one, 0)

    expand(coup_ref, own, left_coef)
    for copy in coup_copies:
        copy.wait()
    expand(call, chosen, right_coef)
    local.wait()

    outs = []
    for t in order:
        start, count = spans[t]

        @pl.when(has_left)
        def _():
            halo(t, True).wait_recv()

        @pl.when(has_right)
        def _():
            halo(t, False).wait_recv()

        def load(e, carry):
            total = None
            for step, factor in weights:
                term = gbuf[e + step, pl.ds(start, per_tile)].reshape(LANES, width) * factor
                total = term if total is None else total + term
            xt[pl.ds(pl.multiple_of(e * width, 8), width), :] = jnp.transpose(total)
            return carry

        lax.fori_loop(0, rows, load, 0)

        def times_right(b, carry):
            held = jnp.stack([xt[pl.ds(b * orb + d, 8, stride=cells), :] for d in range(orb)])
            for f in range(orb):
                mid[f * orb + b] = jnp.sum(right_coef[t, f * orb : (f + 1) * orb] * held, axis=0)
            return carry

        lax.fori_loop(0, orb, times_right, 0)

        def times_left(f, carry):
            held = mid[pl.ds(f * orb, orb)]
            for a in range(orb):
                ot[pl.ds(a * orb + f, 8, stride=cells), :] = jnp.sum(
                    left_coef[t, a * orb : (a + 1) * orb] * held, axis=0
                )
            return carry

        lax.fori_loop(0, orb, times_left, 0)

        def store(e, carry):
            block = jnp.transpose(ot[pl.ds(pl.multiple_of(e * width, 8), width), :])
            obuf[e, pl.ds(start, per_tile)] = block.reshape(per_tile, atoms, width)
            return carry

        lax.fori_loop(0, rows, store, 0)

        copy = pltpu.make_async_copy(
            obuf.at[:, pl.ds(start, count)], out_ref.at[:, pl.ds(start, count)], out_sem.at[t]
        )
        copy.start()
        outs.append(copy)

    for t in order:

        @pl.when(has_right)
        def _():
            halo(t, True).wait_send()

        @pl.when(has_left)
        def _():
            halo(t, False).wait_send()

    for copy in outs:
        copy.wait()


def local(energy_count, atom_count, green_blocks, coupling, neighbours, freq_offset, emit_weight, absorb_weight):
    rows, atoms, nbrs, width = green_blocks.shape
    orb = coupling.shape[1]
    tiles = -(-(nbrs * atoms) // LANES)
    padded = tiles * LANES // atoms
    vmem = pl.BlockSpec(memory_space=pltpu.VMEM)
    anywhere = pl.BlockSpec(memory_space=pl.ANY)
    f32 = jnp.float32
    result = pl.pallas_call(
        functools.partial(kernel, energy_count, atom_count),
        out_shape=jax.ShapeDtypeStruct((rows, nbrs, atoms, width), f32),
        in_specs=[anywhere, vmem, vmem, vmem, vmem, vmem],
        out_specs=anywhere,
        scratch_shapes=[
            pltpu.VMEM((rows + 2 * OFF, padded, atoms, width), f32),
            pltpu.VMEM((rows, padded, atoms, width), f32),
            pltpu.VMEM((orb, atoms * atom_count, orb), f32),
            pltpu.VMEM((tiles, orb * orb, 8, LANES), f32),
            pltpu.VMEM((tiles, orb * orb, 8, LANES), f32),
            pltpu.VMEM((rows * width, LANES), f32),
            pltpu.VMEM((orb * orb, 8, LANES), f32),
            pltpu.VMEM((rows * width, LANES), f32),
            pltpu.SemaphoreType.DMA,
            pltpu.SemaphoreType.DMA((tiles,)),
            pltpu.SemaphoreType.DMA((2, tiles)),
            pltpu.SemaphoreType.DMA((2, tiles)),
            pltpu.SemaphoreType.DMA((max(atom_count - 1, 1),)),
            pltpu.SemaphoreType.DMA((max(atom_count - 1, 1),)),
        ],
        compiler_params=pltpu.CompilerParams(
            collective_id=0, has_side_effects=True, vmem_limit_bytes=48 * 1024 * 1024
        ),
    )(
        jnp.transpose(green_blocks, (0, 2, 1, 3)),
        jnp.transpose(coupling, (1, 0, 2)),
        neighbours,
        freq_offset.reshape(1, -1),
        emit_weight.reshape(1, -1),
        absorb_weight.reshape(1, -1),
    )
    return jnp.transpose(result, (0, 2, 1, 3))


def solution(mesh):
    placed = (
        P("energy", "atom", None, None),
        P("atom", None, None),
        P("atom", None),
        P(),
        P(),
        P(),
    )
    return jax.shard_map(
        functools.partial(local, mesh.shape["energy"], mesh.shape["atom"]),
        mesh=mesh,
        in_specs=placed,
        out_specs=P("energy", "atom", None, None),
        check_vma=False,
    )
```

profile of v0, /device:TPU:25, one launch (start us, length us, event | category | flops | bytes accessed | tf_op | source)
XLA Modules:
  0.0 48.5 jit_solution(9865450168431232655)
XLA Ops:
  0.0 0.0 copy-start
  0.0 1.4 %copy-done = f32[4,8,34,288]{3,1,2,0:T(8,128)S(1)} copy-done((f32[4,8,34,288]{3,1,2,0:T(8,128)S(1)}, f32[4,8,34,288]{3,1,2,0:T(8,128)}, u32[]{:S(2)}) %copy-start) | copy-done | bytes 1253400
  1.4 0.0 copy-start.1
  1.4 0.8 %copy-done.1 = f32[8,12,12]{2,0,1:T(8,128)S(1)} copy-done((f32[8,12,12]{2,0,1:T(8,128)S(1)}, f32[8,12,12]{2,0,1:T(8,128)}, u32[]{:S(2)}) %copy-start.1) | copy-done | bytes 4632
  2.2 0.0 copy-start.2
  2.2 0.7 %copy-done.2 = s32[8,34]{1,0:T(8,128)S(1)} copy-done((s32[8,34]{1,0:T(8,128)S(1)}, s32[8,34]{1,0:T(8,128)}, u32[]{:S(2)}) %copy-start.2) | copy-done | bytes 1112
  2.9 0.0 copy-start.3
  2.9 0.7 %copy-done.3 = s32[64]{0:T(128)S(1)} copy-done((s32[64]{0:T(128)S(1)}, s32[64]{0:T(128)}, u32[]{:S(2)}) %copy-start.3) | copy-done | bytes 280
  3.6 0.0 copy-start.4
  3.6 0.7 %copy-done.4 = f32[64]{0:T(128)S(1)} copy-done((f32[64]{0:T(128)S(1)}, f32[64]{0:T(128)}, u32[]{:S(2)}) %copy-start.4) | copy-done | bytes 280
  4.2 0.0 copy-start.5
  4.2 0.7 %copy-done.5 = f32[64]{0:T(128)S(1)} copy-done((f32[64]{0:T(128)S(1)}, f32[64]{0:T(128)}, u32[]{:S(2)}) %copy-start.5) | copy-done | bytes 280
  4.9 42.5 %shard_map.64 = f32[4,34,8,288]{3,2,1,0:T(8,128)S(1)} custom-call(f32[4,34,8,288]{3,2,1,0:T(8,128)S(1)} %bitcast.7, f32[12,8,12]{2,1,0:T(8,128)S(1)} %bitcast.8, s32[8,34]{1,0:T(8,128)S(1)} %copy-done.2, s32[1,64]{1,0:T(1,128)S(1)} %bitcast.9, f32[1,64]{1,0:T(1,128)S(1)} %bitcast.10, f32[1,64]{1,0:T(1,128)S(1)} %bitcast.11), custom_call_target="tpu_custom_call" | custom-call | tf_op jit(solution)/shard_map/pallas_call | solution.py:252
  47.4 1.2 %copy.8 = f32[4,8,34,288]{3,1,2,0:T(8,128)} copy(f32[4,8,34,288]{3,1,2,0:T(8,128)S(1)} %bitcast.6) | data formatting | bytes 2506752
Async XLA Ops:
  0.0 1.4 %copy-start = (f32[4,8,34,288]{3,1,2,0:T(8,128)S(1)}, f32[4,8,34,288]{3,1,2,0:T(8,128)}, u32[]{:S(2)}) copy-start(f32[4,8,34,288]{3,1,2,0:T(8,128)} %param.6) | copy-start | bytes 3760132
  1.4 0.8 %copy-start.1 = (f32[8,12,12]{2,0,1:T(8,128)S(1)}, f32[8,12,12]{2,0,1:T(8,128)}, u32[]{:S(2)}) copy-start(f32[8,12,12]{2,0,1:T(8,128)} %param.7) | copy-start | bytes 13828
  2.2 0.7 %copy-start.2 = (s32[8,34]{1,0:T(8,128)S(1)}, s32[8,34]{1,0:T(8,128)}, u32[]{:S(2)}) copy-start(s32[8,34]{1,0:T(8,128)} %nbr_ref.1) | copy-start | bytes 3268
  2.9 0.7 %copy-start.3 = (s32[64]{0:T(128)S(1)}, s32[64]{0:T(128)}, u32[]{:S(2)}) copy-start(s32[64]{0:T(128)} %param.9) | copy-start | bytes 772
  3.6 0.7 %copy-start.4 = (f32[64]{0:T(128)S(1)}, f32[64]{0:T(128)}, u32[]{:S(2)}) copy-start(f32[64]{0:T(128)} %param.10) | copy-start | bytes 772
  4.2 0.7 %copy-start.5 = (f32[64]{0:T(128)S(1)}, f32[64]{0:T(128)}, u32[]{:S(2)}) copy-start(f32[64]{0:T(128)} %param.11) | copy-start | bytes 772
where the time goes:
time: 48.8 us; the launch traced here: 48.5 us
  Pallas kernels  42.5 us (87%)
  local copies, waits for them, and re-layouts  6.07 us (12%)
    pallas_call x1, Pallas kernels, local(): pl.pallas_call(functools.partial(kernel, energy_count, atom_count), out_s...  42.5 us
    unnamed x13, local copies, waits for them, and re-layouts  6.07 us

commit v1 on v0

--- a/solution.py
+++ b/solution.py
@@ -16,21 +16,28 @@
     energy_count,
     atom_count,
     x_ref,
+    coup_hbm,
+    nbr_hbm,
+    freq_hbm,
+    emit_hbm,
+    absorb_hbm,
+    out_ref,
     coup_ref,
     nbr_ref,
     freq_ref,
     emit_ref,
     absorb_ref,
-    out_ref,
     gbuf,
     obuf,
+    packed,
+    arrived,
     call,
     right_coef,
     left_coef,
     xt,
     mid,
     ot,
-    local_sem,
+    load_sem,
     out_sem,
     halo_send,
     halo_recv,
@@ -38,12 +45,15 @@
     coup_recv,
 ):
     rows, nbrs, atoms, width = x_ref.shape
-    orb = coup_ref.shape[0]
+    orb = coup_hbm.shape[0]
     cells = orb * orb
     per_tile = LANES // atoms
     tiles = -(-nbrs // per_tile)
     spans = [(t * per_tile, min(per_tile, nbrs - t * per_tile)) for t in range(tiles)]
-    order = sorted(range(tiles), key=lambda t: (spans[t][1], t))
+    order = [0] + sorted(range(1, tiles), key=lambda t: (spans[t][1], t))
+    full = width // LANES * LANES
+    rest = width - full
+    groups = LANES // rest
     all_atoms = atoms * atom_count
 
     me_e = lax.axis_index("energy")
@@ -67,6 +77,21 @@
     partners = [lax.rem(me_a + k, atom_count) for k in range(1, atom_count)]
     for partner in partners:
         greet(me_e, partner)
+    loads = []
+    for k, (src, dst) in enumerate(
+        [
+            (x_ref, gbuf.at[pl.ds(OFF, rows), pl.ds(0, nbrs)]),
+            (coup_hbm, coup_ref),
+            (nbr_hbm, nbr_ref),
+            (freq_hbm, freq_ref),
+            (emit_hbm, emit_ref),
+            (absorb_hbm, absorb_ref),
+        ]
+    ):
+        copy = pltpu.make_async_copy(src, dst, load_sem.at[k])
+        copy.start()
+        loads.append(copy)
+
     inner = jnp.logical_and(has_left, has_right)
 
     @pl.when(inner)
@@ -78,21 +103,47 @@
         pl.semaphore_wait(barrier, atom_count)
 
     def halo(t, to_right):
-        start, count = spans[t]
         src_row, dst_row, side = (rows - OFF, 0, 0) if to_right else (0, rows + OFF, 1)
+        if t == tiles:
+            src = packed.at[pl.ds(src_row, OFF)]
+            dst = arrived.at[pl.ds(side * OFF, OFF)]
+        else:
+            start, count = spans[t]
+            src = x_ref.at[pl.ds(src_row, OFF), pl.ds(start, count), :, pl.ds(0, full)]
+            dst = gbuf.at[pl.ds(dst_row, OFF), pl.ds(start, count), :, pl.ds(0, full)]
         return pltpu.make_async_remote_copy(
-            src_ref=x_ref.at[pl.ds(src_row, OFF), pl.ds(start, count)],
-            dst_ref=gbuf.at[pl.ds(dst_row, OFF), pl.ds(start, count)],
+            src_ref=src,
+            dst_ref=dst,
             send_sem=halo_send.at[side, t],
             recv_sem=halo_recv.at[side, t],
             device_id=(me_e + 1 if to_right else me_e - 1, me_a),
             device_id_type=MESH,
         )
 
+    def send(t):
+        @pl.when(has_right)
+        def _():
+            halo(t, True).start()
+
+        @pl.when(has_left)
+        def _():
+            halo(t, False).start()
+
+    def receive(t):
+        @pl.when(has_left)
+        def _():
+            halo(t, True).wait_recv()
+
+        @pl.when(has_right)
+        def _():
+            halo(t, False).wait_recv()
+
+    send(order[0])
+
     coup_copies = []
     for k, partner in enumerate(partners):
         copy = pltpu.make_async_remote_copy(
-            src_ref=coup_ref,
+            src_ref=coup_hbm,
             dst_ref=call.at[:, pl.ds(pl.multiple_of(me_a * atoms, atoms), atoms)],
             send_sem=coup_send.at[k],
             recv_sem=coup_recv.at[k],
@@ -102,28 +153,34 @@
         copy.start()
         coup_copies.append(copy)
 
-    for t in order:
-
-        @pl.when(has_right)
-        def _():
-            halo(t, True).start()
-
-        @pl.when(has_left)
-        def _():
-            halo(t, False).start()
-
-    local = pltpu.make_async_copy(x_ref, gbuf.at[pl.ds(OFF, rows), pl.ds(0, nbrs)], local_sem)
-    local.start()
-
+    loads[0].wait()
+    gbuf[OFF : OFF + rows, nbrs:] = jnp.zeros((rows, gbuf.shape[1] - nbrs) + gbuf.shape[2:], jnp.float32)
+
+    def pack(m, carry):
+        for e in range(rows):
+            packed[e, m] = jnp.concatenate(
+                [gbuf[OFF + e, m * groups + k, :, full:] for k in range(groups)], axis=-1
+            )
+        return carry
+
+    lax.fori_loop(0, packed.shape[1], pack, 0)
+    send(tiles)
+    for t in order[1:]:
+        send(t)
+
+    for copy in loads[1:]:
+        copy.wait()
     call[:, pl.ds(pl.multiple_of(me_a * atoms, atoms), atoms), :] = coup_ref[...]
 
     @pl.when(jnp.logical_not(has_left))
     def _():
         gbuf[0:OFF] = jnp.zeros((OFF,) + gbuf.shape[1:], jnp.float32)
+        arrived[0:OFF] = jnp.zeros((OFF,) + arrived.shape[1:], jnp.float32)
 
     @pl.when(jnp.logical_not(has_right))
     def _():
         gbuf[rows + OFF : rows + 2 * OFF] = jnp.zeros((OFF,) + gbuf.shape[1:], jnp.float32)
+        arrived[OFF : 2 * OFF] = jnp.zeros((OFF,) + arrived.shape[1:], jnp.float32)
 
     freq = freq_ref[...]
 
@@ -172,62 +229,65 @@
     for copy in coup_copies:
         copy.wait()
     expand(call, chosen, right_coef)
-    local.wait()
+
+    def unpack(m, carry):
+        for row in range(2 * OFF):
+            piece = arrived[row, m]
+            target = row if row < OFF else rows + row
+            for k in range(groups):
+                gbuf[target, m * groups + k, :, full:] = piece[:, k * rest : (k + 1) * rest]
+        return carry
 
     outs = []
-    for t in order:
+    for place, t in enumerate(order):
         start, count = spans[t]
-
-        @pl.when(has_left)
-        def _():
-            halo(t, True).wait_recv()
-
-        @pl.when(has_right)
-        def _():
-            halo(t, False).wait_recv()
-
-        def load(e, carry):
+        receive(t)
+        if place == 0:
+            receive(tiles)
+            lax.fori_loop(0, packed.shape[1], unpack, 0)
+
+        for e in range(rows):
             total = None
             for step, factor in weights:
                 term = gbuf[e + step, pl.ds(start, per_tile)].reshape(LANES, width) * factor
                 total = term if total is None else total + term
-            xt[pl.ds(pl.multiple_of(e * width, 8), width), :] = jnp.transpose(total)
+            xt[e * width : (e + 1) * width, :] = jnp.transpose(total)
+
+        def times_right(pair, carry):
+            first = pair * 2
+            held = [
+                jnp.stack([xt[pl.ds((first + k) * orb + d, 8, stride=cells), :] for d in range(orb)])
+                for k in range(2)
+            ]
+            for f in range(orb):
+                factor = right_coef[t, f * orb : (f + 1) * orb]
+                for k in range(2):
+                    mid[f * orb + first + k] = jnp.sum(factor * held[k], axis=0)
             return carry
 
-        lax.fori_loop(0, rows, load, 0)
-
-        def times_right(b, carry):
-            held = jnp.stack([xt[pl.ds(b * orb + d, 8, stride=cells), :] for d in range(orb)])
-            for f in range(orb):
-                mid[f * orb + b] = jnp.sum(right_coef[t, f * orb : (f + 1) * orb] * held, axis=0)
+        lax.fori_loop(0, orb // 2, times_right, 0)
+
+        def times_left(pair, carry):
+            first = pair * 2
+            held = [mid[pl.ds((first + k) * orb, orb)] for k in range(2)]
+            for a in range(orb):
+                factor = left_coef[t, a * orb : (a + 1) * orb]
+                for k in range(2):
+                    ot[pl.ds(a * orb + first + k, 8, stride=cells), :] = jnp.sum(factor * held[k], axis=0)
             return carry
 
-        lax.fori_loop(0, orb, times_right, 0)
-
-        def times_left(f, carry):
-            held = mid[pl.ds(f * orb, orb)]
-            for a in range(orb):
-                ot[pl.ds(a * orb + f, 8, stride=cells), :] = jnp.sum(
-                    left_coef[t, a * orb : (a + 1) * orb] * held, axis=0
-                )
-            return carry
-
-        lax.fori_loop(0, orb, times_left, 0)
-
-        def store(e, carry):
-            block = jnp.transpose(ot[pl.ds(pl.multiple_of(e * width, 8), width), :])
-            obuf[e, pl.ds(start, per_tile)] = block.reshape(per_tile, atoms, width)
-            return carry
-
-        lax.fori_loop(0, rows, store, 0)
-
+        lax.fori_loop(0, orb // 2, times_left, 0)
+
+        for e in range(rows):
+            block = jnp.transpose(ot[e * width : (e + 1) * width, :])
+            obuf[e, start : start + per_tile] = block.reshape(per_tile, atoms, width)
         copy = pltpu.make_async_copy(
             obuf.at[:, pl.ds(start, count)], out_ref.at[:, pl.ds(start, count)], out_sem.at[t]
         )
         copy.start()
         outs.append(copy)
 
-    for t in order:
+    for t in range(tiles + 1):
 
         @pl.when(has_right)
         def _():
@@ -246,32 +306,39 @@
     orb = coupling.shape[1]
     tiles = -(-(nbrs * atoms) // LANES)
     padded = tiles * LANES // atoms
-    vmem = pl.BlockSpec(memory_space=pltpu.VMEM)
-    anywhere = pl.BlockSpec(memory_space=pl.ANY)
+    hbm = pl.BlockSpec(memory_space=pltpu.HBM)
+    left_over = LANES // (width % LANES)
     f32 = jnp.float32
     result = pl.pallas_call(
         functools.partial(kernel, energy_count, atom_count),
         out_shape=jax.ShapeDtypeStruct((rows, nbrs, atoms, width), f32),
-        in_specs=[anywhere, vmem, vmem, vmem, vmem, vmem],
-        out_specs=anywhere,
+        in_specs=[hbm] * 6,
+        out_specs=hbm,
         scratch_shapes=[
+            pltpu.VMEM((orb, atoms, orb), f32),
+            pltpu.VMEM((atoms, nbrs), jnp.int32),
+            pltpu.VMEM((1, freq_offset.shape[0]), jnp.int32),
+            pltpu.VMEM((1, freq_offset.shape[0]), f32),
+            pltpu.VMEM((1, freq_offset.shape[0]), f32),
             pltpu.VMEM((rows + 2 * OFF, padded, atoms, width), f32),
             pltpu.VMEM((rows, padded, atoms, width), f32),
+            pltpu.VMEM((rows, -(-nbrs // left_over), atoms, LANES), f32),
+            pltpu.VMEM((2 * OFF, -(-nbrs // left_over), atoms, LANES), f32),
             pltpu.VMEM((orb, atoms * atom_count, orb), f32),
             pltpu.VMEM((tiles, orb * orb, 8, LANES), f32),
             pltpu.VMEM((tiles, orb * orb, 8, LANES), f32),
             pltpu.VMEM((rows * width, LANES), f32),
             pltpu.VMEM((orb * orb, 8, LANES), f32),
             pltpu.VMEM((rows * width, LANES), f32),
-            pltpu.SemaphoreType.DMA,
+            pltpu.SemaphoreType.DMA((6,)),
             pltpu.SemaphoreType.DMA((tiles,)),
-            pltpu.SemaphoreType.DMA((2, tiles)),
-            pltpu.SemaphoreType.DMA((2, tiles)),
+            pltpu.SemaphoreType.DMA((2, tiles + 1)),
+            pltpu.SemaphoreType.DMA((2, tiles + 1)),
             pltpu.SemaphoreType.DMA((max(atom_count - 1, 1),)),
             pltpu.SemaphoreType.DMA((max(atom_count - 1, 1),)),
         ],
         compiler_params=pltpu.CompilerParams(
-            collective_id=0, has_side_effects=True, vmem_limit_bytes=48 * 1024 * 1024
+            collective_id=0, has_side_effects=True, vmem_limit_bytes=64 * 1024 * 1024
         ),
     )(
         jnp.transpose(green_blocks, (0, 2, 1, 3)),

time: 48.8 us -> 37.2 us (0.76)
  Pallas kernels: 42.5 us -> 34.3 us
  local copies, waits for them, and re-layouts: 6.07 us -> 2.72 us
    pallas_call x1, Pallas kernels: 42.5 us -> 34.3 us  [local(): pl.pallas_call(functools.partial(kernel, energy_count, atom_count), out_s...]
    unnamed x13 -> x1, local copies, waits for them, and re-layouts: 6.07 us -> 2.72 us
where the time goes in v1:
time: 37.2 us; the launch traced here: 37 us
  Pallas kernels  34.3 us (92%)
  local copies, waits for them, and re-layouts  2.72 us (7%)
    pallas_call x1, Pallas kernels, local(): pl.pallas_call(functools.partial(kernel, energy_count, atom_count), out_s...  34.3 us
    unnamed x1, local copies, waits for them, and re-layouts  2.72 us

profile of v1, /device:TPU:25, one launch (start us, length us, event | category | flops | bytes accessed | tf_op | source)
XLA Modules:
  0.0 37.0 jit_solution(10926019503535872117)
XLA Ops:
  0.0 34.3 %shard_map.64 = f32[4,34,8,288]{3,2,1,0:T(8,128)} custom-call(f32[4,34,8,288]{3,2,1,0:T(8,128)} %bitcast.7, f32[12,8,12]{2,1,0:T(8,128)} %bitcast.8, s32[8,34]{1,0:T(8,128)} %nbr_hbm.1, s32[1,64]{1,0:T(1,128)} %bitcast.9, f32[1,64]{1,0:T(1,128)} %bitcast.10, f32[1,64]{1,0:T(1,128)} %bitcast.11), custom_call_target="tpu_custom_call" | custom-call | tf_op jit(solution)/shard_map/pallas_call | solution.py:312
  34.3 2.7 %copy.8 = f32[4,8,34,288]{3,1,2,0:T(8,128)} copy(f32[4,8,34,288]{3,1,2,0:T(8,128)} %bitcast.6) | data formatting | bytes 2506752

commit v2 on v1

--- a/solution.py
+++ b/solution.py
@@ -8,6 +8,7 @@
 from jax.sharding import PartitionSpec as P
 
 OFF = 2
+RELAYED = 3
 LANES = 128
 MESH = pl.DeviceIdType.MESH
 
@@ -28,9 +29,9 @@
     emit_ref,
     absorb_ref,
     gbuf,
-    obuf,
     packed,
     arrived,
+    relay,
     call,
     right_coef,
     left_coef,
@@ -38,9 +39,10 @@
     mid,
     ot,
     load_sem,
-    out_sem,
     halo_send,
     halo_recv,
+    relay_send,
+    relay_recv,
     coup_send,
     coup_recv,
 ):
@@ -55,6 +57,9 @@
     rest = width - full
     groups = LANES // rest
     all_atoms = atoms * atom_count
+    half = per_tile // 2
+    pieces = [(start, min(half, nbrs - start)) for start in range(0, nbrs, half)]
+    held_by = {t: [p for p, (start, _) in enumerate(pieces) if start // per_tile == t] for t in range(tiles)}
 
     me_e = lax.axis_index("energy")
     me_a = lax.axis_index("atom")
@@ -73,6 +78,14 @@
     @pl.when(has_right)
     def _():
         greet(me_e + 1, me_a)
+
+    @pl.when(me_e > 1)
+    def _():
+        greet(me_e - 2, me_a)
+
+    @pl.when(me_e < energy_count - 2)
+    def _():
+        greet(me_e + 2, me_a)
 
     partners = [lax.rem(me_a + k, atom_count) for k in range(1, atom_count)]
     for partner in partners:
@@ -92,53 +105,118 @@
         copy.start()
         loads.append(copy)
 
-    inner = jnp.logical_and(has_left, has_right)
-
-    @pl.when(inner)
+    outer = jnp.logical_or(me_e == 0, me_e == energy_count - 1)
+    beside = jnp.logical_or(me_e == 1, me_e == energy_count - 2)
+
+    @pl.when(outer)
     def _():
         pl.semaphore_wait(barrier, atom_count + 1)
 
-    @pl.when(jnp.logical_not(inner))
-    def _():
-        pl.semaphore_wait(barrier, atom_count)
-
-    def halo(t, to_right):
+    @pl.when(beside)
+    def _():
+        pl.semaphore_wait(barrier, atom_count + 2)
+
+    @pl.when(jnp.logical_not(jnp.logical_or(outer, beside)))
+    def _():
+        pl.semaphore_wait(barrier, atom_count + 3)
+
+    def halo(p, to_right):
         src_row, dst_row, side = (rows - OFF, 0, 0) if to_right else (0, rows + OFF, 1)
-        if t == tiles:
+        if p == len(pieces):
             src = packed.at[pl.ds(src_row, OFF)]
             dst = arrived.at[pl.ds(side * OFF, OFF)]
         else:
-            start, count = spans[t]
+            start, count = pieces[p]
             src = x_ref.at[pl.ds(src_row, OFF), pl.ds(start, count), :, pl.ds(0, full)]
             dst = gbuf.at[pl.ds(dst_row, OFF), pl.ds(start, count), :, pl.ds(0, full)]
         return pltpu.make_async_remote_copy(
             src_ref=src,
             dst_ref=dst,
-            send_sem=halo_send.at[side, t],
-            recv_sem=halo_recv.at[side, t],
+            send_sem=halo_send.at[side, p],
+            recv_sem=halo_recv.at[side, p],
             device_id=(me_e + 1 if to_right else me_e - 1, me_a),
             device_id_type=MESH,
         )
 
-    def send(t):
+    pairs = energy_count // 2
+    mine = lax.div(me_e, 2)
+    odd = lax.rem(me_e, 2) == 1
+    even = lax.rem(me_e, 2) == 0
+    via_right = lax.div((RELAYED + 1) * (pairs - 1 - mine), pairs)
+    via_left = lax.div((RELAYED + 1) * mine, pairs)
+
+    def detour(p, to_right):
+        start, count = pieces[p]
+        src_row, side = (rows - OFF, 0) if to_right else (0, 1)
+        return pltpu.make_async_remote_copy(
+            src_ref=x_ref.at[pl.ds(src_row, OFF), pl.ds(start, count), :, pl.ds(0, full)],
+            dst_ref=relay.at[p],
+            send_sem=halo_send.at[side, p],
+            recv_sem=relay_recv.at[p],
+            device_id=(me_e - 1 if to_right else me_e + 1, me_a),
+            device_id_type=MESH,
+        )
+
+    def passed_on(p, to_right):
+        start, count = pieces[p]
+        dst_row, side = (0, 0) if to_right else (rows + OFF, 1)
+        return pltpu.make_async_remote_copy(
+            src_ref=relay.at[p],
+            dst_ref=gbuf.at[pl.ds(dst_row, OFF), pl.ds(start, count), :, pl.ds(0, full)],
+            send_sem=relay_send.at[p],
+            recv_sem=halo_recv.at[side, p],
+            device_id=(me_e + 2 if to_right else me_e - 2, me_a),
+            device_id_type=MESH,
+        )
+
+    def send(p):
+        if p < RELAYED:
+            around_right = jnp.logical_and(odd, p < via_right)
+            around_left = jnp.logical_and(even, p < via_left)
+
+            @pl.when(around_right)
+            def _():
+                detour(p, True).start()
+
+            @pl.when(around_left)
+            def _():
+                detour(p, False).start()
+
+            straight_right = jnp.logical_and(has_right, jnp.logical_not(around_right))
+            straight_left = jnp.logical_and(has_left, jnp.logical_not(around_left))
+        else:
+            straight_right, straight_left = has_right, has_left
+
+        @pl.when(straight_right)
+        def _():
+            halo(p, True).start()
+
+        @pl.when(straight_left)
+        def _():
+            halo(p, False).start()
+
+    def forward(p):
+        @pl.when(jnp.logical_and(odd, p < via_left))
+        def _():
+            detour(p, False).wait_recv()
+            passed_on(p, False).start()
+
+        @pl.when(jnp.logical_and(even, p < via_right))
+        def _():
+            detour(p, True).wait_recv()
+            passed_on(p, True).start()
+
+    def receive(p):
+        @pl.when(has_left)
+        def _():
+            halo(p, True).wait_recv()
+
         @pl.when(has_right)
         def _():
-            halo(t, True).start()
-
-        @pl.when(has_left)
-        def _():
-            halo(t, False).start()
-
-    def receive(t):
-        @pl.when(has_left)
-        def _():
-            halo(t, True).wait_recv()
-
-        @pl.when(has_right)
-        def _():
-            halo(t, False).wait_recv()
-
-    send(order[0])
+            halo(p, False).wait_recv()
+
+    for p in held_by[order[0]]:
+        send(p)
 
     coup_copies = []
     for k, partner in enumerate(partners):
@@ -164,9 +242,10 @@
         return carry
 
     lax.fori_loop(0, packed.shape[1], pack, 0)
-    send(tiles)
+    send(len(pieces))
     for t in order[1:]:
-        send(t)
+        for p in held_by[t]:
+            send(p)
 
     for copy in loads[1:]:
         copy.wait()
@@ -226,9 +305,12 @@
         lax.fori_loop(0, orb, one, 0)
 
     expand(coup_ref, own, left_coef)
+    forward(0)
     for copy in coup_copies:
         copy.wait()
     expand(call, chosen, right_coef)
+    for p in range(1, RELAYED - 1):
+        forward(p)
 
     def unpack(m, carry):
         for row in range(2 * OFF):
@@ -238,12 +320,14 @@
                 gbuf[target, m * groups + k, :, full:] = piece[:, k * rest : (k + 1) * rest]
         return carry
 
-    outs = []
     for place, t in enumerate(order):
         start, count = spans[t]
-        receive(t)
+        if place == 1:
+            forward(RELAYED - 1)
+        for p in held_by[t]:
+            receive(p)
         if place == 0:
-            receive(tiles)
+            receive(len(pieces))
             lax.fori_loop(0, packed.shape[1], unpack, 0)
 
         for e in range(rows):
@@ -280,25 +364,27 @@
 
         for e in range(rows):
             block = jnp.transpose(ot[e * width : (e + 1) * width, :])
-            obuf[e, start : start + per_tile] = block.reshape(per_tile, atoms, width)
-        copy = pltpu.make_async_copy(
-            obuf.at[:, pl.ds(start, count)], out_ref.at[:, pl.ds(start, count)], out_sem.at[t]
-        )
-        copy.start()
-        outs.append(copy)
-
-    for t in range(tiles + 1):
+            out_ref[e, start : start + count] = block[: count * atoms].reshape(count, atoms, width)
+
+    for p in range(len(pieces) + 1):
 
         @pl.when(has_right)
         def _():
-            halo(t, True).wait_send()
+            halo(p, True).wait_send()
 
         @pl.when(has_left)
         def _():
-            halo(t, False).wait_send()
-
-    for copy in outs:
-        copy.wait()
+            halo(p, False).wait_send()
+
+    for p in range(RELAYED):
+
+        @pl.when(jnp.logical_and(odd, p < via_left))
+        def _():
+            passed_on(p, False).wait_send()
+
+        @pl.when(jnp.logical_and(even, p < via_right))
+        def _():
+            passed_on(p, True).wait_send()
 
 
 def local(energy_count, atom_count, green_blocks, coupling, neighbours, freq_offset, emit_weight, absorb_weight):
@@ -307,13 +393,14 @@
     tiles = -(-(nbrs * atoms) // LANES)
     padded = tiles * LANES // atoms
     hbm = pl.BlockSpec(memory_space=pltpu.HBM)
+    piece_count = -(-nbrs // (LANES // atoms // 2))
     left_over = LANES // (width % LANES)
     f32 = jnp.float32
     result = pl.pallas_call(
         functools.partial(kernel, energy_count, atom_count),
-        out_shape=jax.ShapeDtypeStruct((rows, nbrs, atoms, width), f32),
+        out_shape=pltpu.VMEM((rows, nbrs, atoms, width), f32),
         in_specs=[hbm] * 6,
-        out_specs=hbm,
+        out_specs=pl.BlockSpec(memory_space=pltpu.VMEM),
         scratch_shapes=[
             pltpu.VMEM((orb, atoms, orb), f32),
             pltpu.VMEM((atoms, nbrs), jnp.int32),
@@ -321,9 +408,9 @@
             pltpu.VMEM((1, freq_offset.shape[0]), f32),
             pltpu.VMEM((1, freq_offset.shape[0]), f32),
             pltpu.VMEM((rows + 2 * OFF, padded, atoms, width), f32),
-            pltpu.VMEM((rows, padded, atoms, width), f32),
             pltpu.VMEM((rows, -(-nbrs // left_over), atoms, LANES), f32),
             pltpu.VMEM((2 * OFF, -(-nbrs // left_over), atoms, LANES), f32),
+            pltpu.VMEM((RELAYED, OFF, LANES // atoms // 2, atoms, width // LANES * LANES), f32),
             pltpu.VMEM((orb, atoms * atom_count, orb), f32),
             pltpu.VMEM((tiles, orb * orb, 8, LANES), f32),
             pltpu.VMEM((tiles, orb * orb, 8, LANES), f32),
@@ -331,22 +418,28 @@
             pltpu.VMEM((orb * orb, 8, LANES), f32),
             pltpu.VMEM((rows * width, LANES), f32),
             pltpu.SemaphoreType.DMA((6,)),
-            pltpu.SemaphoreType.DMA((tiles,)),
-            pltpu.SemaphoreType.DMA((2, tiles + 1)),
-            pltpu.SemaphoreType.DMA((2, tiles + 1)),
+            pltpu.SemaphoreType.DMA((2, piece_count + 1)),
+            pltpu.SemaphoreType.DMA((2, piece_count + 1)),
+            pltpu.SemaphoreType.DMA((RELAYED,)),
+            pltpu.SemaphoreType.DMA((RELAYED,)),
             pltpu.SemaphoreType.DMA((max(atom_count - 1, 1),)),
             pltpu.SemaphoreType.DMA((max(atom_count - 1, 1),)),
         ],
         compiler_params=pltpu.CompilerParams(
-            collective_id=0, has_side_effects=True, vmem_limit_bytes=64 * 1024 * 1024
+            collective_id=0, has_side_effects=True, vmem_limit_bytes=48 * 1024 * 1024
         ),
     )(
-        jnp.transpose(green_blocks, (0, 2, 1, 3)),
-        jnp.transpose(coupling, (1, 0, 2)),
-        neighbours,
-        freq_offset.reshape(1, -1),
-        emit_weight.reshape(1, -1),
-        absorb_weight.reshape(1, -1),
+        *(
+            pltpu.with_memory_space_constraint(operand, pltpu.HBM)
+            for operand in (
+                jnp.transpose(green_blocks, (0, 2, 1, 3)),
+                jnp.transpose(coupling, (1, 0, 2)),
+                neighbours,
+                freq_offset.reshape(1, -1),
+                emit_weight.reshape(1, -1),
+                absorb_weight.reshape(1, -1),
+            )
+        )
     )
     return jnp.transpose(result, (0, 2, 1, 3))
 

time: 37.2 us -> 32 us (0.86)
  Pallas kernels: 34.3 us -> 30.7 us
  local copies, waits for them, and re-layouts: 2.72 us -> 1.18 us
    pallas_call x1, Pallas kernels: 34.3 us -> 30.7 us  [local(): pl.pallas_call(functools.partial(kernel, energy_count, atom_count), out_s...]
    unnamed x1, local copies, waits for them, and re-layouts: 2.72 us -> 1.18 us
where the time goes in v2:
time: 32 us; the launch traced here: 31.9 us
  Pallas kernels  30.7 us (96%)
  local copies, waits for them, and re-layouts  1.18 us (4%)
    pallas_call x1, Pallas kernels, local(): pl.pallas_call(functools.partial(kernel, energy_count, atom_count), out_s...  30.7 us
    unnamed x1, local copies, waits for them, and re-layouts  1.18 us

profile of v2, /device:TPU:25, one launch (start us, length us, event | category | flops | bytes accessed | tf_op | source)
XLA Modules:
  0.0 31.9 jit_solution(6014243494898008916)
XLA Ops:
  0.0 30.7 %shard_map.64 = f32[4,34,8,288]{3,2,1,0:T(8,128)S(1)} custom-call(f32[4,34,8,288]{3,2,1,0:T(8,128)} %bitcast.7, f32[12,8,12]{2,1,0:T(8,128)} %bitcast.8, s32[8,34]{1,0:T(8,128)} %nbr_hbm.1, s32[1,64]{1,0:T(1,128)} %bitcast.9, f32[1,64]{1,0:T(1,128)} %bitcast.10, f32[1,64]{1,0:T(1,128)} %bitcast.11), custom_call_target="tpu_custom_call" | custom-call | tf_op jit(solution)/shard_map/pallas_call | solution.py:399
  30.7 1.2 %copy.8 = f32[4,8,34,288]{3,1,2,0:T(8,128)} copy(f32[4,8,34,288]{3,1,2,0:T(8,128)S(1)} %bitcast.6) | data formatting | bytes 2506752

commit v3 on v2

--- a/solution.py
+++ b/solution.py
@@ -52,10 +52,10 @@
     per_tile = LANES // atoms
     tiles = -(-nbrs // per_tile)
     spans = [(t * per_tile, min(per_tile, nbrs - t * per_tile)) for t in range(tiles)]
-    order = [0] + sorted(range(1, tiles), key=lambda t: (spans[t][1], t))
     full = width // LANES * LANES
     rest = width - full
     groups = LANES // rest
+    packs = [(t * per_tile // groups, -(-(spans[t][0] + spans[t][1]) // groups) - t * per_tile // groups) for t in range(tiles)]
     all_atoms = atoms * atom_count
     half = per_tile // 2
     pieces = [(start, min(half, nbrs - start)) for start in range(0, nbrs, half)]
@@ -120,14 +120,20 @@
     def _():
         pl.semaphore_wait(barrier, atom_count + 3)
 
+    def own_rows(p, row):
+        start, count = pieces[p]
+        ref, row = (x_ref, row) if start < per_tile else (gbuf, row + OFF)
+        return ref.at[pl.ds(row, OFF), pl.ds(start, count), :, pl.ds(0, full)]
+
     def halo(p, to_right):
         src_row, dst_row, side = (rows - OFF, 0, 0) if to_right else (0, rows + OFF, 1)
-        if p == len(pieces):
-            src = packed.at[pl.ds(src_row, OFF)]
-            dst = arrived.at[pl.ds(side * OFF, OFF)]
+        if p >= len(pieces):
+            first, count = packs[p - len(pieces)]
+            src = packed.at[pl.ds(src_row, OFF), pl.ds(first, count)]
+            dst = arrived.at[pl.ds(side * OFF, OFF), pl.ds(first, count)]
         else:
             start, count = pieces[p]
-            src = x_ref.at[pl.ds(src_row, OFF), pl.ds(start, count), :, pl.ds(0, full)]
+            src = own_rows(p, src_row)
             dst = gbuf.at[pl.ds(dst_row, OFF), pl.ds(start, count), :, pl.ds(0, full)]
         return pltpu.make_async_remote_copy(
             src_ref=src,
@@ -146,10 +152,9 @@
     via_left = lax.div((RELAYED + 1) * mine, pairs)
 
     def detour(p, to_right):
-        start, count = pieces[p]
         src_row, side = (rows - OFF, 0) if to_right else (0, 1)
         return pltpu.make_async_remote_copy(
-            src_ref=x_ref.at[pl.ds(src_row, OFF), pl.ds(start, count), :, pl.ds(0, full)],
+            src_ref=own_rows(p, src_row),
             dst_ref=relay.at[p],
             send_sem=halo_send.at[side, p],
             recv_sem=relay_recv.at[p],
@@ -215,7 +220,7 @@
         def _():
             halo(p, False).wait_recv()
 
-    for p in held_by[order[0]]:
+    for p in held_by[0]:
         send(p)
 
     coup_copies = []
@@ -234,18 +239,20 @@
     loads[0].wait()
     gbuf[OFF : OFF + rows, nbrs:] = jnp.zeros((rows, gbuf.shape[1] - nbrs) + gbuf.shape[2:], jnp.float32)
 
-    def pack(m, carry):
-        for e in range(rows):
-            packed[e, m] = jnp.concatenate(
-                [gbuf[OFF + e, m * groups + k, :, full:] for k in range(groups)], axis=-1
-            )
-        return carry
-
-    lax.fori_loop(0, packed.shape[1], pack, 0)
-    send(len(pieces))
-    for t in order[1:]:
-        for p in held_by[t]:
-            send(p)
+    def send_packed(t):
+        first, count = packs[t]
+
+        def pack(m, carry):
+            for e in range(rows):
+                packed[e, m] = jnp.concatenate(
+                    [gbuf[OFF + e, m * groups + k, :, full:] for k in range(groups)], axis=-1
+                )
+            return carry
+
+        lax.fori_loop(first, first + count, pack, 0)
+        send(len(pieces) + t)
+
+    send_packed(0)
 
     for copy in loads[1:]:
         copy.wait()
@@ -302,40 +309,16 @@
                     target[t, a * orb + d] = jnp.broadcast_to(row, (8, LANES))
             return carry
 
-        lax.fori_loop(0, orb, one, 0)
+        lax.fori_loop(0, orb, one, 0, unroll=4)
 
     expand(coup_ref, own, left_coef)
-    forward(0)
     for copy in coup_copies:
         copy.wait()
     expand(call, chosen, right_coef)
-    for p in range(1, RELAYED - 1):
-        forward(p)
-
-    def unpack(m, carry):
-        for row in range(2 * OFF):
-            piece = arrived[row, m]
-            target = row if row < OFF else rows + row
-            for k in range(groups):
-                gbuf[target, m * groups + k, :, full:] = piece[:, k * rest : (k + 1) * rest]
-        return carry
-
-    for place, t in enumerate(order):
-        start, count = spans[t]
-        if place == 1:
-            forward(RELAYED - 1)
-        for p in held_by[t]:
-            receive(p)
-        if place == 0:
-            receive(len(pieces))
-            lax.fori_loop(0, packed.shape[1], unpack, 0)
-
+
+    def dress(t, read, write):
         for e in range(rows):
-            total = None
-            for step, factor in weights:
-                term = gbuf[e + step, pl.ds(start, per_tile)].reshape(LANES, width) * factor
-                total = term if total is None else total + term
-            xt[e * width : (e + 1) * width, :] = jnp.transpose(total)
+            xt[e * width : (e + 1) * width, :] = jnp.transpose(read(e))
 
         def times_right(pair, carry):
             first = pair * 2
@@ -363,10 +346,63 @@
         lax.fori_loop(0, orb // 2, times_left, 0)
 
         for e in range(rows):
-            block = jnp.transpose(ot[e * width : (e + 1) * width, :])
-            out_ref[e, start : start + count] = block[: count * atoms].reshape(count, atoms, width)
-
-    for p in range(len(pieces) + 1):
+            write(e, jnp.transpose(ot[e * width : (e + 1) * width, :]))
+
+    def filtered(e, start, count):
+        total = None
+        for step, factor in weights:
+            term = gbuf[e + step, pl.ds(start, count)].reshape(count * atoms, width) * factor
+            total = term if total is None else total + term
+        return total
+
+    def receive_packed(t):
+        first, count = packs[t]
+        receive(len(pieces) + t)
+
+        def unpack(m, carry):
+            for row in range(2 * OFF):
+                piece = arrived[row, m]
+                target = row if row < OFF else rows + row
+                for k in range(groups):
+                    gbuf[target, m * groups + k, :, full:] = piece[:, k * rest : (k + 1) * rest]
+            return carry
+
+        lax.fori_loop(first, first + count, unpack, 0)
+
+    for t in range(1, tiles):
+        start, count = spans[t]
+
+        def write(e, block):
+            gbuf[OFF + e, start : start + per_tile] = block.reshape(per_tile, atoms, width)
+
+        dress(t, lambda e: gbuf[OFF + e, start : start + per_tile].reshape(LANES, width), write)
+        for p in held_by[t]:
+            send(p)
+        send_packed(t)
+        forward(t - 1)
+
+    for p in range(tiles - 1, RELAYED - 1):
+        forward(p)
+    for p in held_by[0]:
+        receive(p)
+    receive_packed(0)
+
+    def write_first(e, block):
+        count = spans[0][1]
+        out_ref[e, :count] = block[: count * atoms].reshape(count, atoms, width)
+
+    dress(0, lambda e: filtered(e, 0, per_tile), write_first)
+    forward(RELAYED - 1)
+
+    for t in range(1, tiles):
+        receive_packed(t)
+        for p in held_by[t]:
+            start, count = pieces[p]
+            receive(p)
+            for e in range(rows):
+                out_ref[e, start : start + count] = filtered(e, start, count).reshape(count, atoms, width)
+
+    for p in range(len(pieces) + tiles):
 
         @pl.when(has_right)
         def _():
@@ -418,8 +454,8 @@
             pltpu.VMEM((orb * orb, 8, LANES), f32),
             pltpu.VMEM((rows * width, LANES), f32),
             pltpu.SemaphoreType.DMA((6,)),
-            pltpu.SemaphoreType.DMA((2, piece_count + 1)),
-            pltpu.SemaphoreType.DMA((2, piece_count + 1)),
+            pltpu.SemaphoreType.DMA((2, piece_count + tiles)),
+            pltpu.SemaphoreType.DMA((2, piece_count + tiles)),
             pltpu.SemaphoreType.DMA((RELAYED,)),
             pltpu.SemaphoreType.DMA((RELAYED,)),
             pltpu.SemaphoreType.DMA((max(atom_count - 1, 1),)),

time: 32 us -> 30.5 us (0.953)
  Pallas kernels: 30.7 us -> 29.1 us
    pallas_call x1, Pallas kernels: 30.7 us -> 29.1 us  [local(): pl.pallas_call(functools.partial(kernel, energy_count, atom_count), out_s...]
where the time goes in v3:
time: 30.5 us; the launch traced here: 30.3 us
  Pallas kernels  29.1 us (95%)
  local copies, waits for them, and re-layouts  1.18 us (4%)
    pallas_call x1, Pallas kernels, local(): pl.pallas_call(functools.partial(kernel, energy_count, atom_count), out_s...  29.1 us
    unnamed x1, local copies, waits for them, and re-layouts  1.18 us

profile of v3, /device:TPU:25, one launch (start us, length us, event | category | flops | bytes accessed | tf_op | source)
XLA Modules:
  0.0 30.3 jit_solution(2349315868709575800)
XLA Ops:
  0.0 29.1 %shard_map.64 = f32[4,34,8,288]{3,2,1,0:T(8,128)S(1)} custom-call(f32[4,34,8,288]{3,2,1,0:T(8,128)} %bitcast.7, f32[12,8,12]{2,1,0:T(8,128)} %bitcast.8, s32[8,34]{1,0:T(8,128)} %nbr_hbm.1, s32[1,64]{1,0:T(1,128)} %bitcast.9, f32[1,64]{1,0:T(1,128)} %bitcast.10, f32[1,64]{1,0:T(1,128)} %bitcast.11), custom_call_target="tpu_custom_call" | custom-call | tf_op jit(solution)/shard_map/pallas_call | solution.py:435
  29.2 1.2 %copy.8 = f32[4,8,34,288]{3,1,2,0:T(8,128)} copy(f32[4,8,34,288]{3,1,2,0:T(8,128)S(1)} %bitcast.6) | data formatting | bytes 2506752

commit v4 on v3

--- a/solution.py
+++ b/solution.py
@@ -56,6 +56,8 @@
     rest = width - full
     groups = LANES // rest
     packs = [(t * per_tile // groups, -(-(spans[t][0] + spans[t][1]) // groups) - t * per_tile // groups) for t in range(tiles)]
+    raw = [t for t in range(tiles) if t == 0 or spans[t][1] < per_tile]
+    owned = [t for t in range(tiles) if t not in raw]
     all_atoms = atoms * atom_count
     half = per_tile // 2
     pieces = [(start, min(half, nbrs - start)) for start in range(0, nbrs, half)]
@@ -105,6 +107,34 @@
         copy.start()
         loads.append(copy)
 
+    for copy in loads[1:]:
+        copy.wait()
+    freq = freq_ref[...]
+
+    def weight(ref, step):
+        return jnp.sum(jnp.where(freq == step, ref[...], 0.0), axis=1, keepdims=True)
+
+    weights = [
+        (0, weight(emit_ref, 2)),
+        (1, weight(emit_ref, 1)),
+        (3, weight(absorb_ref, 1)),
+        (4, weight(absorb_ref, 2)),
+    ]
+
+    lanes = tiles * LANES
+    slot = lax.broadcasted_iota(jnp.int32, (nbrs, lanes), 0)
+    pair = lax.broadcasted_iota(jnp.int32, (nbrs, lanes), 1)
+    spread = jnp.where(pair // atoms == slot, 1.0, 0.0).astype(jnp.float32)
+    listed = jnp.dot(
+        nbr_ref[...].astype(jnp.float32), spread, preferred_element_type=jnp.float32, precision=lax.Precision.HIGHEST
+    )
+    atom_row = lax.broadcasted_iota(jnp.int32, (atoms, lanes), 0)
+    atom_pair = lax.broadcasted_iota(jnp.int32, (atoms, lanes), 1)
+    own = jnp.where(atom_pair % atoms == atom_row, 1.0, 0.0).astype(jnp.float32)
+    index = jnp.sum(listed * own, axis=0, keepdims=True)
+    ids = lax.broadcasted_iota(jnp.int32, (all_atoms, lanes), 0).astype(jnp.float32)
+    chosen = jnp.where(ids == index, 1.0, 0.0).astype(jnp.float32)
+
     outer = jnp.logical_or(me_e == 0, me_e == energy_count - 1)
     beside = jnp.logical_or(me_e == 1, me_e == energy_count - 2)
 
@@ -122,7 +152,7 @@
 
     def own_rows(p, row):
         start, count = pieces[p]
-        ref, row = (x_ref, row) if start < per_tile else (gbuf, row + OFF)
+        ref, row = (x_ref, row) if start // per_tile in raw else (gbuf, row + OFF)
         return ref.at[pl.ds(row, OFF), pl.ds(start, count), :, pl.ds(0, full)]
 
     def halo(p, to_right):
@@ -220,9 +250,6 @@
         def _():
             halo(p, False).wait_recv()
 
-    for p in held_by[0]:
-        send(p)
-
     coup_copies = []
     for k, partner in enumerate(partners):
         copy = pltpu.make_async_remote_copy(
@@ -236,6 +263,10 @@
         copy.start()
         coup_copies.append(copy)
 
+    for t in raw:
+        for p in held_by[t]:
+            send(p)
+
     loads[0].wait()
     gbuf[OFF : OFF + rows, nbrs:] = jnp.zeros((rows, gbuf.shape[1] - nbrs) + gbuf.shape[2:], jnp.float32)
 
@@ -252,10 +283,9 @@
         lax.fori_loop(first, first + count, pack, 0)
         send(len(pieces) + t)
 
-    send_packed(0)
-
-    for copy in loads[1:]:
-        copy.wait()
+    for t in raw:
+        send_packed(t)
+
     call[:, pl.ds(pl.multiple_of(me_a * atoms, atoms), atoms), :] = coup_ref[...]
 
     @pl.when(jnp.logical_not(has_left))
@@ -268,53 +298,27 @@
         gbuf[rows + OFF : rows + 2 * OFF] = jnp.zeros((OFF,) + gbuf.shape[1:], jnp.float32)
         arrived[OFF : 2 * OFF] = jnp.zeros((OFF,) + arrived.shape[1:], jnp.float32)
 
-    freq = freq_ref[...]
-
-    def weight(ref, step):
-        return jnp.sum(jnp.where(freq == step, ref[...], 0.0), axis=1, keepdims=True)
-
-    weights = [
-        (0, weight(emit_ref, 2)),
-        (1, weight(emit_ref, 1)),
-        (3, weight(absorb_ref, 1)),
-        (4, weight(absorb_ref, 2)),
-    ]
-
-    lanes = tiles * LANES
-    slot = lax.broadcasted_iota(jnp.int32, (nbrs, lanes), 0)
-    pair = lax.broadcasted_iota(jnp.int32, (nbrs, lanes), 1)
-    spread = jnp.where(pair // atoms == slot, 1.0, 0.0).astype(jnp.float32)
-    listed = jnp.dot(
-        nbr_ref[...].astype(jnp.float32), spread, preferred_element_type=jnp.float32, precision=lax.Precision.HIGHEST
-    )
-    atom_row = lax.broadcasted_iota(jnp.int32, (atoms, lanes), 0)
-    atom_pair = lax.broadcasted_iota(jnp.int32, (atoms, lanes), 1)
-    own = jnp.where(atom_pair % atoms == atom_row, 1.0, 0.0).astype(jnp.float32)
-    index = jnp.sum(listed * own, axis=0, keepdims=True)
-    ids = lax.broadcasted_iota(jnp.int32, (all_atoms, lanes), 0).astype(jnp.float32)
-    chosen = jnp.where(ids == index, 1.0, 0.0).astype(jnp.float32)
-
-    def expand(source, select, target):
+    def expand(source, select, target, t):
         def one(a, carry):
             table = lax.dot_general(
                 source[a],
-                select,
+                select[:, t * LANES : (t + 1) * LANES],
                 (((0,), (0,)), ((), ())),
                 preferred_element_type=jnp.float32,
                 precision=lax.Precision.HIGHEST,
             )
-            for t in range(tiles):
-                for d in range(orb):
-                    row = table[d : d + 1, t * LANES : (t + 1) * LANES]
-                    target[t, a * orb + d] = jnp.broadcast_to(row, (8, LANES))
+            for d in range(orb):
+                target[t, a * orb + d] = jnp.broadcast_to(table[d : d + 1], (8, LANES))
             return carry
 
         lax.fori_loop(0, orb, one, 0, unroll=4)
 
-    expand(coup_ref, own, left_coef)
+    for t in owned:
+        expand(coup_ref, own, left_coef, t)
     for copy in coup_copies:
         copy.wait()
-    expand(call, chosen, right_coef)
+    for t in owned:
+        expand(call, chosen, right_coef, t)
 
     def dress(t, read, write):
         for e in range(rows):
@@ -369,7 +373,7 @@
 
         lax.fori_loop(first, first + count, unpack, 0)
 
-    for t in range(1, tiles):
+    for t in owned:
         start, count = spans[t]
 
         def write(e, block):
@@ -379,22 +383,28 @@
         for p in held_by[t]:
             send(p)
         send_packed(t)
-        forward(t - 1)
-
-    for p in range(tiles - 1, RELAYED - 1):
+
+    forward(0)
+    for t in raw:
+        expand(coup_ref, own, left_coef, t)
+        expand(call, chosen, right_coef, t)
+    for p in range(1, RELAYED - 1):
         forward(p)
-    for p in held_by[0]:
-        receive(p)
-    receive_packed(0)
-
-    def write_first(e, block):
-        count = spans[0][1]
-        out_ref[e, :count] = block[: count * atoms].reshape(count, atoms, width)
-
-    dress(0, lambda e: filtered(e, 0, per_tile), write_first)
-    forward(RELAYED - 1)
-
-    for t in range(1, tiles):
+
+    for place, t in enumerate(raw):
+        start, count = spans[t]
+
+        def write(e, block):
+            out_ref[e, start : start + count] = block[: count * atoms].reshape(count, atoms, width)
+
+        for p in held_by[t]:
+            receive(p)
+        receive_packed(t)
+        dress(t, lambda e: filtered(e, start, per_tile), write)
+        if place == 0:
+            forward(RELAYED - 1)
+
+    for t in owned:
         receive_packed(t)
         for p in held_by[t]:
             start, count = pieces[p]

time: 30.5 us -> 30.9 us (1.013)
  Pallas kernels: 29.1 us -> 29.5 us
    pallas_call x1, Pallas kernels: 29.1 us -> 29.5 us  [local(): pl.pallas_call(functools.partial(kernel, energy_count, atom_count), out_s...]
where the time goes in v4:
time: 30.9 us; the launch traced here: 30.7 us
  Pallas kernels  29.5 us (95%)
  local copies, waits for them, and re-layouts  1.18 us (4%)
    pallas_call x1, Pallas kernels, local(): pl.pallas_call(functools.partial(kernel, energy_count, atom_count), out_s...  29.5 us
    unnamed x1, local copies, waits for them, and re-layouts  1.18 us

profile of v4, /device:TPU:25, one launch (start us, length us, event | category | flops | bytes accessed | tf_op | source)
XLA Modules:
  0.0 30.7 jit_solution(2303257495449258761)
XLA Ops:
  0.0 29.5 %shard_map.64 = f32[4,34,8,288]{3,2,1,0:T(8,128)S(1)} custom-call(f32[4,34,8,288]{3,2,1,0:T(8,128)} %bitcast.7, f32[12,8,12]{2,1,0:T(8,128)} %bitcast.8, s32[8,34]{1,0:T(8,128)} %nbr_hbm.1, s32[1,64]{1,0:T(1,128)} %bitcast.9, f32[1,64]{1,0:T(1,128)} %bitcast.10, f32[1,64]{1,0:T(1,128)} %bitcast.11), custom_call_target="tpu_custom_call" | custom-call | tf_op jit(solution)/shard_map/pallas_call | solution.py:445
  29.6 1.2 %copy.8 = f32[4,8,34,288]{3,1,2,0:T(8,128)} copy(f32[4,8,34,288]{3,1,2,0:T(8,128)S(1)} %bitcast.6) | data formatting | bytes 2506752

commit v5 on v4

--- a/solution.py
+++ b/solution.py
@@ -28,7 +28,8 @@
     freq_ref,
     emit_ref,
     absorb_ref,
-    gbuf,
+    gmain,
+    grest,
     packed,
     arrived,
     relay,
@@ -95,7 +96,8 @@
     loads = []
     for k, (src, dst) in enumerate(
         [
-            (x_ref, gbuf.at[pl.ds(OFF, rows), pl.ds(0, nbrs)]),
+            (x_ref.at[:, :, :, pl.ds(0, full)], gmain.at[pl.ds(OFF, rows), pl.ds(0, nbrs)]),
+            (x_ref.at[:, :, :, pl.ds(full, rest)], grest.at[pl.ds(OFF, rows), pl.ds(0, nbrs)]),
             (coup_hbm, coup_ref),
             (nbr_hbm, nbr_ref),
             (freq_hbm, freq_ref),
@@ -107,7 +109,7 @@
         copy.start()
         loads.append(copy)
 
-    for copy in loads[1:]:
+    for copy in loads[2:]:
         copy.wait()
     freq = freq_ref[...]
 
@@ -152,8 +154,7 @@
 
     def own_rows(p, row):
         start, count = pieces[p]
-        ref, row = (x_ref, row) if start // per_tile in raw else (gbuf, row + OFF)
-        return ref.at[pl.ds(row, OFF), pl.ds(start, count), :, pl.ds(0, full)]
+        return gmain.at[pl.ds(row + OFF, OFF), pl.ds(start, count)]
 
     def halo(p, to_right):
         src_row, dst_row, side = (rows - OFF, 0, 0) if to_right else (0, rows + OFF, 1)
@@ -164,7 +165,7 @@
         else:
             start, count = pieces[p]
             src = own_rows(p, src_row)
-            dst = gbuf.at[pl.ds(dst_row, OFF), pl.ds(start, count), :, pl.ds(0, full)]
+            dst = gmain.at[pl.ds(dst_row, OFF), pl.ds(start, count)]
         return pltpu.make_async_remote_copy(
             src_ref=src,
             dst_ref=dst,
@@ -197,7 +198,7 @@
         dst_row, side = (0, 0) if to_right else (rows + OFF, 1)
         return pltpu.make_async_remote_copy(
             src_ref=relay.at[p],
-            dst_ref=gbuf.at[pl.ds(dst_row, OFF), pl.ds(start, count), :, pl.ds(0, full)],
+            dst_ref=gmain.at[pl.ds(dst_row, OFF), pl.ds(start, count)],
             send_sem=relay_send.at[p],
             recv_sem=halo_recv.at[side, p],
             device_id=(me_e + 2 if to_right else me_e - 2, me_a),
@@ -263,12 +264,14 @@
         copy.start()
         coup_copies.append(copy)
 
+    loads[0].wait()
     for t in raw:
         for p in held_by[t]:
             send(p)
 
-    loads[0].wait()
-    gbuf[OFF : OFF + rows, nbrs:] = jnp.zeros((rows, gbuf.shape[1] - nbrs) + gbuf.shape[2:], jnp.float32)
+    loads[1].wait()
+    for ref in (gmain, grest):
+        ref[OFF : OFF + rows, nbrs:] = jnp.zeros((rows, ref.shape[1] - nbrs) + ref.shape[2:], jnp.float32)
 
     def send_packed(t):
         first, count = packs[t]
@@ -276,7 +279,7 @@
         def pack(m, carry):
             for e in range(rows):
                 packed[e, m] = jnp.concatenate(
-                    [gbuf[OFF + e, m * groups + k, :, full:] for k in range(groups)], axis=-1
+                    [grest[OFF + e, m * groups + k] for k in range(groups)], axis=-1
                 )
             return carry
 
@@ -290,12 +293,13 @@
 
     @pl.when(jnp.logical_not(has_left))
     def _():
-        gbuf[0:OFF] = jnp.zeros((OFF,) + gbuf.shape[1:], jnp.float32)
-        arrived[0:OFF] = jnp.zeros((OFF,) + arrived.shape[1:], jnp.float32)
+        for ref in (gmain, grest, arrived):
+            ref[0:OFF] = jnp.zeros((OFF,) + ref.shape[1:], jnp.float32)
 
     @pl.when(jnp.logical_not(has_right))
     def _():
-        gbuf[rows + OFF : rows + 2 * OFF] = jnp.zeros((OFF,) + gbuf.shape[1:], jnp.float32)
+        for ref in (gmain, grest):
+            ref[rows + OFF : rows + 2 * OFF] = jnp.zeros((OFF,) + ref.shape[1:], jnp.float32)
         arrived[OFF : 2 * OFF] = jnp.zeros((OFF,) + arrived.shape[1:], jnp.float32)
 
     def expand(source, select, target, t):
@@ -322,7 +326,8 @@
 
     def dress(t, read, write):
         for e in range(rows):
-            xt[e * width : (e + 1) * width, :] = jnp.transpose(read(e))
+            for base, block in zip((0, full), read(e)):
+                xt[e * width + base : e * width + base + block.shape[1], :] = jnp.transpose(block)
 
         def times_right(pair, carry):
             first = pair * 2
@@ -350,14 +355,30 @@
         lax.fori_loop(0, orb // 2, times_left, 0)
 
         for e in range(rows):
-            write(e, jnp.transpose(ot[e * width : (e + 1) * width, :]))
+            write(
+                e,
+                [
+                    jnp.transpose(ot[e * width : e * width + full, :]),
+                    jnp.transpose(ot[e * width + full : (e + 1) * width, :]),
+                ],
+            )
+
+    def rows_of(row, start, count):
+        return [ref[row, pl.ds(start, count)].reshape(count * atoms, ref.shape[3]) for ref in (gmain, grest)]
 
     def filtered(e, start, count):
-        total = None
+        totals = None
         for step, factor in weights:
-            term = gbuf[e + step, pl.ds(start, count)].reshape(count * atoms, width) * factor
-            total = term if total is None else total + term
-        return total
+            terms = [part * factor for part in rows_of(e + step, start, count)]
+            totals = terms if totals is None else [total + term for total, term in zip(totals, terms)]
+        return totals
+
+    def write_out(e, start, count, blocks):
+        for base, block in zip((0, full), blocks):
+            size = block.shape[1]
+            out_ref[e, start : start + count, :, base : base + size] = block[: count * atoms].reshape(
+                count, atoms, size
+            )
 
     def receive_packed(t):
         first, count = packs[t]
@@ -368,7 +389,7 @@
                 piece = arrived[row, m]
                 target = row if row < OFF else rows + row
                 for k in range(groups):
-                    gbuf[target, m * groups + k, :, full:] = piece[:, k * rest : (k + 1) * rest]
+                    grest[target, m * groups + k] = piece[:, k * rest : (k + 1) * rest]
             return carry
 
         lax.fori_loop(first, first + count, unpack, 0)
@@ -376,10 +397,11 @@
     for t in owned:
         start, count = spans[t]
 
-        def write(e, block):
-            gbuf[OFF + e, start : start + per_tile] = block.reshape(per_tile, atoms, width)
-
-        dress(t, lambda e: gbuf[OFF + e, start : start + per_tile].reshape(LANES, width), write)
+        def write(e, blocks):
+            for ref, block in zip((gmain, grest), blocks):
+                ref[OFF + e, start : start + per_tile] = block.reshape(per_tile, atoms, block.shape[1])
+
+        dress(t, lambda e: rows_of(OFF + e, start, per_tile), write)
         for p in held_by[t]:
             send(p)
         send_packed(t)
@@ -394,13 +416,10 @@
     for place, t in enumerate(raw):
         start, count = spans[t]
 
-        def write(e, block):
-            out_ref[e, start : start + count] = block[: count * atoms].reshape(count, atoms, width)
-
         for p in held_by[t]:
             receive(p)
         receive_packed(t)
-        dress(t, lambda e: filtered(e, start, per_tile), write)
+        dress(t, lambda e: filtered(e, start, per_tile), lambda e, blocks: write_out(e, start, count, blocks))
         if place == 0:
             forward(RELAYED - 1)
 
@@ -410,7 +429,7 @@
             start, count = pieces[p]
             receive(p)
             for e in range(rows):
-                out_ref[e, start : start + count] = filtered(e, start, count).reshape(count, atoms, width)
+                write_out(e, start, count, filtered(e, start, count))
 
     for p in range(len(pieces) + tiles):
 
@@ -453,7 +472,8 @@
             pltpu.VMEM((1, freq_offset.shape[0]), jnp.int32),
             pltpu.VMEM((1, freq_offset.shape[0]), f32),
             pltpu.VMEM((1, freq_offset.shape[0]), f32),
-            pltpu.VMEM((rows + 2 * OFF, padded, atoms, width), f32),
+            pltpu.VMEM((rows + 2 * OFF, padded, atoms, width // LANES * LANES), f32),
+            pltpu.VMEM((rows + 2 * OFF, padded, atoms, width % LANES), f32),
             pltpu.VMEM((rows, -(-nbrs // left_over), atoms, LANES), f32),
             pltpu.VMEM((2 * OFF, -(-nbrs // left_over), atoms, LANES), f32),
             pltpu.VMEM((RELAYED, OFF, LANES // atoms // 2, atoms, width // LANES * LANES), f32),
@@ -463,7 +483,7 @@
             pltpu.VMEM((rows * width, LANES), f32),
             pltpu.VMEM((orb * orb, 8, LANES), f32),
             pltpu.VMEM((rows * width, LANES), f32),
-            pltpu.SemaphoreType.DMA((6,)),
+            pltpu.SemaphoreType.DMA((7,)),
             pltpu.SemaphoreType.DMA((2, piece_count + tiles)),
             pltpu.SemaphoreType.DMA((2, piece_count + tiles)),
             pltpu.SemaphoreType.DMA((RELAYED,)),

time: 30.9 us -> 30.7 us (level)
  no operation moved by 1% of the time
where the time goes in v5:
time: 30.7 us; the launch traced here: 30.5 us
  Pallas kernels  29.3 us (95%)
  local copies, waits for them, and re-layouts  1.18 us (4%)
    pallas_call x1, Pallas kernels, local(): pl.pallas_call(functools.partial(kernel, energy_count, atom_count), out_s...  29.3 us
    unnamed x1, local copies, waits for them, and re-layouts  1.18 us

profile of v5, /device:TPU:25, one launch (start us, length us, event | category | flops | bytes accessed | tf_op | source)
XLA Modules:
  0.0 30.5 jit_solution(5485819972842506487)
XLA Ops:
  0.0 29.3 %shard_map.64 = f32[4,34,8,288]{3,2,1,0:T(8,128)S(1)} custom-call(f32[4,34,8,288]{3,2,1,0:T(8,128)} %bitcast.7, f32[12,8,12]{2,1,0:T(8,128)} %bitcast.8, s32[8,34]{1,0:T(8,128)} %nbr_hbm.1, s32[1,64]{1,0:T(1,128)} %bitcast.9, f32[1,64]{1,0:T(1,128)} %bitcast.10, f32[1,64]{1,0:T(1,128)} %bitcast.11), custom_call_target="tpu_custom_call" | custom-call | tf_op jit(solution)/shard_map/pallas_call | solution.py:464
  29.3 1.2 %copy.8 = f32[4,8,34,288]{3,1,2,0:T(8,128)} copy(f32[4,8,34,288]{3,1,2,0:T(8,128)S(1)} %bitcast.6) | data formatting | bytes 2506752

commit v6 on v4

--- a/solution.py
+++ b/solution.py
@@ -8,9 +8,16 @@
 from jax.sharding import PartitionSpec as P
 
 OFF = 2
-RELAYED = 3
+QUARTERS = 4
 LANES = 128
 MESH = pl.DeviceIdType.MESH
+
+
+def tile_spans(nbrs, per_tile, groups):
+    second = (nbrs - per_tile) // 2 // groups * groups
+    spans = [(0, per_tile), (per_tile, second), (per_tile + second, nbrs - per_tile - second)]
+    assert 0 < second and spans[2][1] <= per_tile
+    return spans
 
 
 def kernel(
@@ -32,6 +39,7 @@
     packed,
     arrived,
     relay,
+    relay_packed,
     call,
     right_coef,
     left_coef,
@@ -50,18 +58,19 @@
     orb = coup_hbm.shape[0]
     cells = orb * orb
     per_tile = LANES // atoms
-    tiles = -(-nbrs // per_tile)
-    spans = [(t * per_tile, min(per_tile, nbrs - t * per_tile)) for t in range(tiles)]
+    spans = tile_spans(nbrs, per_tile, LANES // (width % LANES))
+    tiles = len(spans)
     full = width // LANES * LANES
     rest = width - full
     groups = LANES // rest
-    packs = [(t * per_tile // groups, -(-(spans[t][0] + spans[t][1]) // groups) - t * per_tile // groups) for t in range(tiles)]
-    raw = [t for t in range(tiles) if t == 0 or spans[t][1] < per_tile]
-    owned = [t for t in range(tiles) if t not in raw]
+    packs = [(start // groups, -(-(start + count) // groups) - start // groups) for start, count in spans]
+    early = (spans[0][1] + 2) // 2
+    pieces = [(0, early), (early, spans[0][1] - early)] + spans[1:]
+    held_by = {t: [p for p, (start, _) in enumerate(pieces) if spans[t][0] <= start < sum(spans[t])] for t in range(tiles)}
+    level = {0: 1, 2: 2, len(pieces) + 1: 2, 1: 3, len(pieces): 3}
+    raw = list(range(tiles - 1))[::-1]
+    owned = [tiles - 1]
     all_atoms = atoms * atom_count
-    half = per_tile // 2
-    pieces = [(start, min(half, nbrs - start)) for start in range(0, nbrs, half)]
-    held_by = {t: [p for p, (start, _) in enumerate(pieces) if start // per_tile == t] for t in range(tiles)}
 
     me_e = lax.axis_index("energy")
     me_a = lax.axis_index("atom")
@@ -124,7 +133,11 @@
     lanes = tiles * LANES
     slot = lax.broadcasted_iota(jnp.int32, (nbrs, lanes), 0)
     pair = lax.broadcasted_iota(jnp.int32, (nbrs, lanes), 1)
-    spread = jnp.where(pair // atoms == slot, 1.0, 0.0).astype(jnp.float32)
+    listed_slot = pair // atoms
+    for t in range(1, tiles):
+        move = spans[t][0] - t * per_tile
+        listed_slot = jnp.where(pair // LANES == t, pair // atoms + move, listed_slot)
+    spread = jnp.where(listed_slot == slot, 1.0, 0.0).astype(jnp.float32)
     listed = jnp.dot(
         nbr_ref[...].astype(jnp.float32), spread, preferred_element_type=jnp.float32, precision=lax.Precision.HIGHEST
     )
@@ -152,7 +165,7 @@
 
     def own_rows(p, row):
         start, count = pieces[p]
-        ref, row = (x_ref, row) if start // per_tile in raw else (gbuf, row + OFF)
+        ref, row = (x_ref, row) if start < spans[-1][0] else (gbuf, row + OFF)
         return ref.at[pl.ds(row, OFF), pl.ds(start, count), :, pl.ds(0, full)]
 
     def halo(p, to_right):
@@ -178,14 +191,25 @@
     mine = lax.div(me_e, 2)
     odd = lax.rem(me_e, 2) == 1
     even = lax.rem(me_e, 2) == 0
-    via_right = lax.div((RELAYED + 1) * (pairs - 1 - mine), pairs)
-    via_left = lax.div((RELAYED + 1) * mine, pairs)
+    via_right = lax.div(QUARTERS * (pairs - 1 - mine), pairs)
+    via_left = lax.div(QUARTERS * mine, pairs)
+
+    def ends_of(p, to_right):
+        src_row, dst_row, side = (rows - OFF, 0, 0) if to_right else (0, rows + OFF, 1)
+        if p >= len(pieces):
+            first, count = packs[p - len(pieces)]
+            src = packed.at[pl.ds(src_row, OFF), pl.ds(first, count)]
+            dst = arrived.at[pl.ds(side * OFF, OFF), pl.ds(first, count)]
+            return src, relay_packed.at[:, pl.ds(first, count)], dst, side
+        start, count = pieces[p]
+        dst = gbuf.at[pl.ds(dst_row, OFF), pl.ds(start, count), :, pl.ds(0, full)]
+        return own_rows(p, src_row), relay.at[:, pl.ds(start, count)], dst, side
 
     def detour(p, to_right):
-        src_row, side = (rows - OFF, 0) if to_right else (0, 1)
+        src, middle, _, side = ends_of(p, to_right)
         return pltpu.make_async_remote_copy(
-            src_ref=own_rows(p, src_row),
-            dst_ref=relay.at[p],
+            src_ref=src,
+            dst_ref=middle,
             send_sem=halo_send.at[side, p],
             recv_sem=relay_recv.at[p],
             device_id=(me_e - 1 if to_right else me_e + 1, me_a),
@@ -193,11 +217,10 @@
         )
 
     def passed_on(p, to_right):
-        start, count = pieces[p]
-        dst_row, side = (0, 0) if to_right else (rows + OFF, 1)
+        _, middle, dst, side = ends_of(p, to_right)
         return pltpu.make_async_remote_copy(
-            src_ref=relay.at[p],
-            dst_ref=gbuf.at[pl.ds(dst_row, OFF), pl.ds(start, count), :, pl.ds(0, full)],
+            src_ref=middle,
+            dst_ref=dst,
             send_sem=relay_send.at[p],
             recv_sem=halo_recv.at[side, p],
             device_id=(me_e + 2 if to_right else me_e - 2, me_a),
@@ -205,9 +228,9 @@
         )
 
     def send(p):
-        if p < RELAYED:
-            around_right = jnp.logical_and(odd, p < via_right)
-            around_left = jnp.logical_and(even, p < via_left)
+        if p in level:
+            around_right = jnp.logical_and(odd, via_right >= level[p])
+            around_left = jnp.logical_and(even, via_left >= level[p])
 
             @pl.when(around_right)
             def _():
@@ -231,12 +254,12 @@
             halo(p, False).start()
 
     def forward(p):
-        @pl.when(jnp.logical_and(odd, p < via_left))
+        @pl.when(jnp.logical_and(odd, via_left >= level[p]))
         def _():
             detour(p, False).wait_recv()
             passed_on(p, False).start()
 
-        @pl.when(jnp.logical_and(even, p < via_right))
+        @pl.when(jnp.logical_and(even, via_right >= level[p]))
         def _():
             detour(p, True).wait_recv()
             passed_on(p, True).start()
@@ -263,9 +286,8 @@
         copy.start()
         coup_copies.append(copy)
 
-    for t in raw:
-        for p in held_by[t]:
-            send(p)
+    for p in sorted((p for p in level if p < len(pieces)), key=level.get):
+        send(p)
 
     loads[0].wait()
     gbuf[OFF : OFF + rows, nbrs:] = jnp.zeros((rows, gbuf.shape[1] - nbrs) + gbuf.shape[2:], jnp.float32)
@@ -322,7 +344,10 @@
 
     def dress(t, read, write):
         for e in range(rows):
-            xt[e * width : (e + 1) * width, :] = jnp.transpose(read(e))
+            block = read(e)
+            if block.shape[0] < LANES:
+                block = jnp.concatenate([block, jnp.zeros((LANES - block.shape[0], width), jnp.float32)], axis=0)
+            xt[e * width : (e + 1) * width, :] = jnp.transpose(block)
 
         def times_right(pair, carry):
             first = pair * 2
@@ -377,9 +402,9 @@
         start, count = spans[t]
 
         def write(e, block):
-            gbuf[OFF + e, start : start + per_tile] = block.reshape(per_tile, atoms, width)
-
-        dress(t, lambda e: gbuf[OFF + e, start : start + per_tile].reshape(LANES, width), write)
+            gbuf[OFF + e, start : start + count] = block[: count * atoms].reshape(count, atoms, width)
+
+        dress(t, lambda e: gbuf[OFF + e, start : start + count].reshape(count * atoms, width), write)
         for p in held_by[t]:
             send(p)
         send_packed(t)
@@ -388,21 +413,20 @@
     for t in raw:
         expand(coup_ref, own, left_coef, t)
         expand(call, chosen, right_coef, t)
-    for p in range(1, RELAYED - 1):
-        forward(p)
-
-    for place, t in enumerate(raw):
+
+    for t in raw:
         start, count = spans[t]
 
         def write(e, block):
             out_ref[e, start : start + count] = block[: count * atoms].reshape(count, atoms, width)
 
+        for p in level:
+            if p > 0 and (p in held_by[t] or p == len(pieces) + t):
+                forward(p)
         for p in held_by[t]:
             receive(p)
         receive_packed(t)
-        dress(t, lambda e: filtered(e, start, per_tile), write)
-        if place == 0:
-            forward(RELAYED - 1)
+        dress(t, lambda e: filtered(e, start, count), write)
 
     for t in owned:
         receive_packed(t)
@@ -422,13 +446,13 @@
         def _():
             halo(p, False).wait_send()
 
-    for p in range(RELAYED):
-
-        @pl.when(jnp.logical_and(odd, p < via_left))
+    for p in level:
+
+        @pl.when(jnp.logical_and(odd, via_left >= level[p]))
         def _():
             passed_on(p, False).wait_send()
 
-        @pl.when(jnp.logical_and(even, p < via_right))
+        @pl.when(jnp.logical_and(even, via_right >= level[p]))
         def _():
             passed_on(p, True).wait_send()
 
@@ -436,11 +460,12 @@
 def local(energy_count, atom_count, green_blocks, coupling, neighbours, freq_offset, emit_weight, absorb_weight):
     rows, atoms, nbrs, width = green_blocks.shape
     orb = coupling.shape[1]
-    tiles = -(-(nbrs * atoms) // LANES)
+    left_over = LANES // (width % LANES)
+    spans = tile_spans(nbrs, LANES // atoms, left_over)
+    tiles = len(spans)
     padded = tiles * LANES // atoms
     hbm = pl.BlockSpec(memory_space=pltpu.HBM)
-    piece_count = -(-nbrs // (LANES // atoms // 2))
-    left_over = LANES // (width % LANES)
+    piece_count = tiles + 1
     f32 = jnp.float32
     result = pl.pallas_call(
         functools.partial(kernel, energy_count, atom_count),
@@ -456,7 +481,8 @@
             pltpu.VMEM((rows + 2 * OFF, padded, atoms, width), f32),
             pltpu.VMEM((rows, -(-nbrs // left_over), atoms, LANES), f32),
             pltpu.VMEM((2 * OFF, -(-nbrs // left_over), atoms, LANES), f32),
-            pltpu.VMEM((RELAYED, OFF, LANES // atoms // 2, atoms, width // LANES * LANES), f32),
+            pltpu.VMEM((OFF, spans[-1][0], atoms, width // LANES * LANES), f32),
+            pltpu.VMEM((OFF, spans[-1][0] // left_over, atoms, LANES), f32),
             pltpu.VMEM((orb, atoms * atom_count, orb), f32),
             pltpu.VMEM((tiles, orb * orb, 8, LANES), f32),
             pltpu.VMEM((tiles, orb * orb, 8, LANES), f32),
@@ -466,8 +492,8 @@
             pltpu.SemaphoreType.DMA((6,)),
             pltpu.SemaphoreType.DMA((2, piece_count + tiles)),
             pltpu.SemaphoreType.DMA((2, piece_count + tiles)),
-            pltpu.SemaphoreType.DMA((RELAYED,)),
-            pltpu.SemaphoreType.DMA((RELAYED,)),
+            pltpu.SemaphoreType.DMA((piece_count + tiles,)),
+            pltpu.SemaphoreType.DMA((piece_count + tiles,)),
             pltpu.SemaphoreType.DMA((max(atom_count - 1, 1),)),
             pltpu.SemaphoreType.DMA((max(atom_count - 1, 1),)),
         ],

time: 30.9 us -> 32.1 us (1.039)
  the two profiles are of different devices: /device:TPU:25 before, /device:TPU:22 now
where the time goes in v6:
time: 32.1 us; the launch traced here: 31.9 us
  Pallas kernels  30.8 us (96%)
  local copies, waits for them, and re-layouts  1.18 us (4%)
    pallas_call x1, Pallas kernels, local(): pl.pallas_call(functools.partial(kernel, energy_count, atom_count), out_s...  30.8 us
    unnamed x1, local copies, waits for them, and re-layouts  1.18 us

profile of v6, /device:TPU:22, one launch (start us, length us, event | category | flops | bytes accessed | tf_op | source)
XLA Modules:
  0.0 31.9 jit_solution(8355111056271111605)
XLA Ops:
  0.0 30.8 %shard_map.64 = f32[4,34,8,288]{3,2,1,0:T(8,128)S(1)} custom-call(f32[4,34,8,288]{3,2,1,0:T(8,128)} %bitcast.7, f32[12,8,12]{2,1,0:T(8,128)} %bitcast.8, s32[8,34]{1,0:T(8,128)} %nbr_hbm.1, s32[1,64]{1,0:T(1,128)} %bitcast.9, f32[1,64]{1,0:T(1,128)} %bitcast.10, f32[1,64]{1,0:T(1,128)} %bitcast.11), custom_call_target="tpu_custom_call" | custom-call | tf_op jit(solution)/shard_map/pallas_call | solution.py:470
  30.8 1.2 %copy.8 = f32[4,8,34,288]{3,1,2,0:T(8,128)} copy(f32[4,8,34,288]{3,1,2,0:T(8,128)S(1)} %bitcast.6) | data formatting | bytes 2506752

commit v7 on v6

--- a/solution.py
+++ b/solution.py
@@ -414,15 +414,16 @@
         expand(coup_ref, own, left_coef, t)
         expand(call, chosen, right_coef, t)
 
+    for p in level:
+        if p > 0:
+            forward(p)
+
     for t in raw:
         start, count = spans[t]
 
         def write(e, block):
             out_ref[e, start : start + count] = block[: count * atoms].reshape(count, atoms, width)
 
-        for p in level:
-            if p > 0 and (p in held_by[t] or p == len(pieces) + t):
-                forward(p)
         for p in held_by[t]:
             receive(p)
         receive_packed(t)

time: 32.1 us -> 32 us (level)
  the two profiles are of different devices: /device:TPU:22 before, /device:TPU:14 now
where the time goes in v7:
time: 32 us; the launch traced here: 31.8 us
  Pallas kernels  30.6 us (96%)
  local copies, waits for them, and re-layouts  1.18 us (4%)
    pallas_call x1, Pallas kernels, local(): pl.pallas_call(functools.partial(kernel, energy_count, atom_count), out_s...  30.6 us
    unnamed x1, local copies, waits for them, and re-layouts  1.18 us

profile of v7, /device:TPU:14, one launch (start us, length us, event | category | flops | bytes accessed | tf_op | source)
XLA Modules:
  0.0 31.8 jit_solution(4488373961232030960)
XLA Ops:
  0.0 30.6 %shard_map.64 = f32[4,34,8,288]{3,2,1,0:T(8,128)S(1)} custom-call(f32[4,34,8,288]{3,2,1,0:T(8,128)} %bitcast.7, f32[12,8,12]{2,1,0:T(8,128)} %bitcast.8, s32[8,34]{1,0:T(8,128)} %nbr_hbm.1, s32[1,64]{1,0:T(1,128)} %bitcast.9, f32[1,64]{1,0:T(1,128)} %bitcast.10, f32[1,64]{1,0:T(1,128)} %bitcast.11), custom_call_target="tpu_custom_call" | custom-call | tf_op jit(solution)/shard_map/pallas_call | solution.py:471
  30.7 1.2 %copy.8 = f32[4,8,34,288]{3,1,2,0:T(8,128)} copy(f32[4,8,34,288]{3,1,2,0:T(8,128)S(1)} %bitcast.6) | data formatting | bytes 2506752
